TPU v7x, 32 devices: a whole 2x2x4 slice. The times are simulated.
32 devices in a mesh: seq: 8 (over z, y), dp: 4 (over x, core).
Axes of the slice: x: 2, y: 2, z: 4, core: 2. Of those that a mesh axis runs over, the one named last changes fastest.
Arguments:
- bases: int32 [98304], P(('dp', 'seq')), parts along dimension 0, may hold values from 0 to 3
- stem_weight: bfloat16 [20, 768], replicated, may hold values from -3 to 3
- stem_gain: float32 [768], replicated, may hold values from 0.5 to 1.5
- first_weight: bfloat16 [5, 768, 896], P(None, None, 'seq'), may hold values from -0.09375 to 0.09375
- first_gain: float32 [896], replicated, may hold values from 0.5 to 1.5
- second_weight: bfloat16 [5, 896, 1024], P(None, None, 'seq'), may hold values from -0.09375 to 0.09375
- second_gain: float32 [1024], replicated, may hold values from 0.5 to 1.5
- bottom_project: bfloat16 [1024, 1024], P(None, 'seq'), may hold values from -0.1875 to 0.1875
- middle_project: bfloat16 [1024, 896], P(None, 'seq'), may hold values from -0.1875 to 0.1875
- top_project: bfloat16 [896, 768], P(None, 'seq'), may hold values from -0.1875 to 0.1875
- head_weight: bfloat16 [768, 5], replicated, may hold values from -0.21875 to 0.21875
Outputs:
- features: bfloat16 [98304, 768], P(('dp', 'seq')), parts along dimension 0
- splice_logits: float32 [5, 98304], P(None, ('dp', 'seq')), parts along dimension 1
There are 4 independent parts, one for each index of `dp`. A program takes and returns all parts, laid end to end along the dimension named above; an argument that names none is the same for every part. Nothing has to cross between parts.
All inputs are finite; a program needn't handle non-finite values.
Results may differ from a plain program's by a relative error of at most 0.015.
Values may be sent and summed in bfloat16 or wider, within the bound.
A program may use at most 192 MiB of HBM per device.

v0:
```python
import functools

import jax
import jax.numpy as jnp
from jax import lax
from jax.experimental import pallas as pl
from jax.experimental.pallas import tpu as pltpu
from jax.sharding import PartitionSpec as P

TAPS = 5
CLASSES = 8
HALO = 16
CHUNK = 32
LANES = 128
PIECE = 1024
BF16 = jnp.bfloat16
F32 = jnp.float32


def gather_kernel(pieces, x_ref, g_ref, local_sem, nat_recv, x_recv, ca_recv, cb_recv,
                  own_send, nat_send, x_send, ca_send, cb_send):
    seq = lax.axis_index("seq")
    dp = lax.axis_index("dp")
    z, y = seq // 2, seq % 2
    x, c = dp // 2, dp % 2
    half, edge, native = PIECE // 2, 3 * PIECE // 16, 5 * PIECE // 16

    def there(zz, yy, xx, cc):
        return {"seq": zz * 2 + yy, "dp": xx * 2 + cc}

    y_dev = there(z, 1 - y, x, c)
    x_dev = there(z, y, 1 - x, c)
    c_dev = there(z, y, x, 1 - c)
    up_dev = there(jnp.minimum(z + 1, 3), y, x, c)
    down_dev = there(jnp.maximum(z - 1, 0), y, x, c)

    barrier = pltpu.get_barrier_semaphore()
    for dev in (y_dev, x_dev, c_dev):
        pl.semaphore_signal(barrier, inc=1, device_id=dev, device_id_type=pl.DeviceIdType.MESH)

    @pl.when(z < 3)
    def _():
        pl.semaphore_signal(barrier, inc=1, device_id=up_dev, device_id_type=pl.DeviceIdType.MESH)

    @pl.when(z > 0)
    def _():
        pl.semaphore_signal(barrier, inc=1, device_id=down_dev, device_id_type=pl.DeviceIdType.MESH)

    inner = jnp.logical_and(z > 0, z < 3)

    @pl.when(inner)
    def _():
        pl.semaphore_wait(barrier, 5)

    @pl.when(jnp.logical_not(inner))
    def _():
        pl.semaphore_wait(barrier, 4)

    def slot(zz, yy, start, count):
        return g_ref.at[zz, pl.ds(pl.multiple_of(start, 64), count),
                        pl.ds(pl.multiple_of(yy * LANES, LANES), LANES)]

    def base(k):
        return k * PIECE + c * half

    def copy(src, dst, send, recv, dev):
        return pltpu.make_async_remote_copy(src_ref=src, dst_ref=dst, send_sem=send, recv_sem=recv,
                                            device_id=dev, device_id_type=pl.DeviceIdType.MESH)

    def nat(k, zz, yy):
        return slot(zz, yy, base(k) + x * edge, native)

    def part(k, zz, yy, xx):
        return slot(zz, yy, base(k) + xx * native, edge)

    def own_copy(k, dev, which):
        src = x_ref.at[pl.ds(pl.multiple_of(base(k) + x * edge, 64), native), :]
        return copy(src, nat(k, z, y), own_send.at[k, which], nat_recv.at[k, seq], dev)

    def z_copy(k, zz, dev):
        s = zz * 2 + y
        return copy(nat(k, zz, y), nat(k, zz, y), nat_send.at[k, 0, zz], nat_recv.at[k, s], dev)

    def y_copy(k, zz):
        s = zz * 2 + y
        return copy(nat(k, zz, y), nat(k, zz, y), nat_send.at[k, 1, zz], nat_recv.at[k, s], y_dev)

    def x_copy(k, zz, yy):
        s = zz * 2 + yy
        return copy(part(k, zz, yy, x), part(k, zz, yy, x), x_send.at[k, s], x_recv.at[k, s], x_dev)

    def ca_copy(k, zz, yy):
        s = zz * 2 + yy
        return copy(nat(k, zz, yy), nat(k, zz, yy), ca_send.at[k, s], ca_recv.at[k, s], c_dev)

    def cb_copy(k, zz, yy):
        s = zz * 2 + yy
        return copy(part(k, zz, yy, 1 - x), part(k, zz, yy, 1 - x), cb_send.at[k, s], cb_recv.at[k, s], c_dev)

    local = pltpu.make_async_copy(
        x_ref, g_ref.at[z, :, pl.ds(pl.multiple_of(y * LANES, LANES), LANES)], local_sem)
    local.start()

    def wait_nat(k, zz, yy):
        pltpu.make_async_copy(nat(k, zz, yy), nat(k, zz, yy), nat_recv.at[k, zz * 2 + yy]).wait()

    def wait_part(k, zz, yy, sem):
        ref = part(k, zz, yy, 1 - x)
        pltpu.make_async_copy(ref, ref, sem.at[k, zz * 2 + yy]).wait()

    def over(body):
        def step(k, carry):
            body(k)
            return carry
        lax.fori_loop(0, pieces, step, 0)

    def when(cond):
        return pl.when(cond)

    def first(k):
        when(z < 3)(lambda: own_copy(k, up_dev, 0).start())
        when(z > 0)(lambda: own_copy(k, down_dev, 1).start())
        own_copy(k, y_dev, 2).start()

    over(first)

    for phase in range(1, 6):
        def body(k, phase=phase):
            if phase <= 3:
                for sign in (-1, 1):
                    zz = z + sign * phase

                    @pl.when(jnp.logical_and(zz >= 0, zz < 4))
                    def _(zz=zz, sign=sign):
                        wait_nat(k, zz, y)
                        if sign < 0:
                            when(z < 3)(lambda: z_copy(k, zz, up_dev).start())
                        else:
                            when(z > 0)(lambda: z_copy(k, zz, down_dev).start())
                        y_copy(k, zz).start()
                        x_copy(k, zz, y).start()
                        ca_copy(k, zz, y).start()
            if phase <= 4:
                for sign in (-1, 1) if phase > 1 else (1,):
                    zz = z + sign * (phase - 1)

                    @pl.when(jnp.logical_and(zz >= 0, zz < 4))
                    def _(zz=zz):
                        wait_nat(k, zz, 1 - y)
                        x_copy(k, zz, 1 - y).start()
                        ca_copy(k, zz, 1 - y).start()
            late = []
            if 2 <= phase <= 4:
                late += [(z - (phase - 1), y), (z + (phase - 1), y)]
            if phase == 2:
                late += [(z, 1 - y)]
            if phase > 2:
                late += [(z - (phase - 2), 1 - y), (z + (phase - 2), 1 - y)]
            for zz, yy in late:
                @pl.when(jnp.logical_and(zz >= 0, zz < 4))
                def _(zz=zz, yy=yy):
                    wait_part(k, zz, yy, x_recv)
                    cb_copy(k, zz, yy).start()

        over(body)

    def last(k):
        when(z < 3)(lambda: own_copy(k, up_dev, 0).wait_send())
        when(z > 0)(lambda: own_copy(k, down_dev, 1).wait_send())
        own_copy(k, y_dev, 2).wait_send()
        for zz in range(4):
            @pl.when(zz != z)
            def _(zz=zz):
                when(jnp.logical_and(zz < z, z < 3))(lambda: z_copy(k, zz, up_dev).wait_send())
                when(jnp.logical_and(zz > z, z > 0))(lambda: z_copy(k, zz, down_dev).wait_send())
                y_copy(k, zz).wait_send()
            for yy in range(2):
                @pl.when(zz * 2 + yy != seq)
                def _(zz=zz, yy=yy):
                    x_copy(k, zz, yy).wait_send()
                    ca_copy(k, zz, yy).wait_send()
                    cb_copy(k, zz, yy).wait_send()
                    start = k * PIECE + (1 - c) * half
                    got = slot(zz, yy, start + x * edge, native)
                    pltpu.make_async_copy(got, got, ca_recv.at[k, zz * 2 + yy]).wait()
                    got = slot(zz, yy, start + (1 - x) * native, edge)
                    pltpu.make_async_copy(got, got, cb_recv.at[k, zz * 2 + yy]).wait()

    over(last)
    local.wait()


def gather_shards(shard):
    rows = shard.shape[0]
    pieces = rows // PIECE
    dma = pltpu.SemaphoreType.DMA
    return pl.pallas_call(
        functools.partial(gather_kernel, pieces),
        out_shape=jax.ShapeDtypeStruct((4, rows, 2 * LANES), shard.dtype),
        in_specs=[pl.BlockSpec(memory_space=pl.ANY)],
        out_specs=pl.BlockSpec(memory_space=pl.ANY),
        scratch_shapes=[dma, dma((pieces, 8)), dma((pieces, 8)), dma((pieces, 8)), dma((pieces, 8)),
                        dma((pieces, 3)), dma((pieces, 2, 4)), dma((pieces, 8)), dma((pieces, 8)), dma((pieces, 8))],
        compiler_params=pltpu.CompilerParams(collective_id=0, has_side_effects=True,
                                             vmem_limit_bytes=16 * 1024 * 1024),
        cost_estimate=pl.CostEstimate(flops=0, bytes_accessed=60_000_000, transcendentals=0),
        name="gather",
    )(shard)


def gelu_norm(values, gain, width):
    square = jnp.sum(values * values, axis=1, keepdims=True) * (1.0 / width)
    v = values * lax.rsqrt(square + 1e-06) * gain
    u = v * (0.7978845608028654 + (0.7978845608028654 * 0.044715) * (v * v))
    h = 0.5 * v
    return h + h * jnp.tanh(u)


def unet_kernel(dims, g_ref, hot_ref, sw_ref, mask_ref, gain0_ref, gain1_ref, gain2_ref, head_ref,
                out_ref, logit_ref, gv, sems, wide, pf, pb1, pb2, skip0, skip1, skip2, mix):
    rows, c0, c1, c2, offs = dims
    ext = rows + 2 * HALO
    w0, w1 = c0 // 8, c1 // 8
    cuts = list(zip(offs[:-1], offs[1:]))

    def load(n):
        lo, hi = cuts[n]
        return pltpu.make_async_copy(g_ref.at[:, pl.ds(lo, hi - lo), :], gv.at[:, pl.ds(lo, hi - lo), :], sems.at[n])

    for n in range(5):
        load(n).start()

    def chunks(count, body):
        def step(i, carry):
            body(pl.multiple_of(i * CHUNK, CHUNK))
            return carry
        lax.fori_loop(0, count // CHUNK, step, 0)

    def shifted(k, start, shift, width):
        if shift == 0:
            return pf[k, pl.ds(start, CHUNK), 0:width].astype(BF16)
        if shift < 0:
            return pf[k, pl.ds(start - 8, CHUNK + 8), 0:width][7:7 + CHUNK].astype(BF16)
        return pf[k, pl.ds(start, CHUNK + 8), 0:width][1:1 + CHUNK].astype(BF16)

    zeros = jnp.zeros((8, pf.shape[2]), F32)
    for k in range(4):
        pf[k, 0:8, :] = zeros
        pf[k, 8 + ext:16 + ext, :] = zeros

    def stem(j, carry):
        for e in range(2):
            wide[e, :, 0:c0] = jnp.dot(hot_ref[...], sw_ref[2 * j + e], preferred_element_type=F32)

        def body(r):
            a0 = gelu_norm(wide[0, pl.ds(r, CHUNK), 0:c0], gain0_ref[...], c0)
            a1 = gelu_norm(wide[1, pl.ds(r, CHUNK), 0:c0], gain0_ref[...], c0)
            skip0[2 * j, pl.ds(r, CHUNK), :] = a0.astype(BF16)
            skip0[2 * j + 1, pl.ds(r, CHUNK), :] = a1.astype(BF16)
            pf[j, pl.ds(r + 8, CHUNK), 0:c0] = 0.5 * (a0 + a1) * mask_ref[pl.ds(r, CHUNK), 0:1]

        chunks(ext, body)
        return carry

    lax.fori_loop(0, 4, stem, 0)

    where1 = {(k, 0): k for k in range(4)} | {(2, -1): 4, (3, -1): 5, (0, 1): 6, (1, 1): 7}
    for (k, shift), at in where1.items():
        def body(r, k=k, shift=shift, at=at):
            pb1[at, pl.ds(r, CHUNK), :] = shifted(k, r + 8, shift, c0)
        chunks(ext, body)

    load(0).wait()
    for j in range(2):
        for e in range(2):
            k = 2 * j + e

            def column(p, carry, k=k, e=e):
                acc = None
                for t in range(TAPS):
                    shift, cls = divmod(k + t - 2, 4)
                    term = jnp.dot(pb1[where1[(cls, shift)]], gv[p, offs[0] + t * c0:offs[0] + (t + 1) * c0, :],
                                   preferred_element_type=F32)
                    acc = term if acc is None else acc + term
                wide[e, :, pl.ds(pl.multiple_of(p * 256, 256), 256)] = acc
                return carry

            lax.fori_loop(0, 4, column, 0)

        def body(r, j=j):
            both = []
            for e in range(2):
                row = wide[e, pl.ds(r, CHUNK), :]
                row = jnp.concatenate([row[:, s * LANES:s * LANES + w1] for s in range(8)], axis=1)
                a = gelu_norm(row, gain1_ref[...], c1)
                skip1[2 * j + e, pl.ds(r, CHUNK), :] = a.astype(BF16)
                both.append(a)
            pf[j, pl.ds(r + 8, CHUNK), 0:c1] = 0.5 * (both[0] + both[1]) * mask_ref[pl.ds(r, CHUNK), 0:1]

        chunks(ext, body)

    where2 = {}
    for k in range(2):
        for shift in (-1, 0, 1):
            at = len(where2)
            where2[(k, shift)] = at

            def body(r, k=k, shift=shift, at=at):
                pb2[at, pl.ds(r, CHUNK), :] = shifted(k, r + 8 + HALO, shift, c1)

            chunks(rows, body)

    load(1).wait()
    for e in range(2):
        def column(p, carry, e=e):
            acc = None
            for t in range(TAPS):
                shift, cls = divmod(e + t - 2, 2)
                term = jnp.dot(pb2[where2[(cls, shift)]], gv[p, offs[1] + t * c1:offs[1] + (t + 1) * c1, :],
                               preferred_element_type=F32)
                acc = term if acc is None else acc + term
            wide[e, 0:rows, pl.ds(pl.multiple_of(p * 256, 256), 256)] = acc
            return carry

        lax.fori_loop(0, 4, column, 0)

    def body(r):
        a0 = gelu_norm(wide[0, pl.ds(r, CHUNK), :], gain2_ref[...], c2)
        a1 = gelu_norm(wide[1, pl.ds(r, CHUNK), :], gain2_ref[...], c2)
        skip2[0, pl.ds(r, CHUNK), :] = a0.astype(BF16)
        skip2[1, pl.ds(r, CHUNK), :] = a1.astype(BF16)
        skip2[2, pl.ds(r, CHUNK), :] = (0.5 * (a0 + a1)).astype(BF16)

    chunks(rows, body)

    def lift(slot, lhs, n, depth):
        def column(p, carry):
            wide[slot, 0:rows, pl.ds(pl.multiple_of(p * 256, 256), 256)] = jnp.dot(
                lhs(), gv[p, offs[n]:offs[n] + depth, :], preferred_element_type=F32)
            return carry
        lax.fori_loop(0, 4, column, 0)

    load(2).wait()
    lift(0, lambda: skip2[2], 2, c2)

    def body(r):
        up = wide[0, pl.ds(r, CHUNK), :]
        for e in range(2):
            skip2[e, pl.ds(r, CHUNK), :] = (skip2[e, pl.ds(r, CHUNK), :].astype(F32) + up).astype(BF16)

    chunks(rows, body)

    load(3).wait()

    def middle(j, carry):
        lift(0, lambda: skip2[j], 3, c2)

        def body(r):
            row = wide[0, pl.ds(r, CHUNK), :]
            up = jnp.concatenate([row[:, s * LANES:s * LANES + w1] for s in range(8)], axis=1)
            for e in range(2):
                at = pl.ds(r + HALO, CHUNK)
                skip1[2 * j + e, at, :] = (skip1[2 * j + e, at, :].astype(F32) + up).astype(BF16)

        chunks(rows, body)
        return carry

    lax.fori_loop(0, 2, middle, 0)

    load(4).wait()

    def top(j, carry):
        lift(0, lambda: skip1[j, HALO:HALO + rows, :], 4, c1)

        def body(r):
            row = wide[0, pl.ds(r, CHUNK), :]
            up = jnp.concatenate([row[:, s * LANES:s * LANES + w0] for s in range(8)], axis=1)
            pf[j, pl.ds(r, CHUNK), 0:c0] = up

        chunks(rows, body)
        return carry

    lax.fori_loop(0, 4, top, 0)

    def final(i, carry):
        r = pl.multiple_of(i * 16, 16)
        for j in range(4):
            up = pf[j, pl.ds(r, 16), 0:c0]
            for e in range(2):
                k = 2 * j + e
                f = skip0[k, pl.ds(r + HALO, 16), :].astype(F32) + up
                for lane in range(0, c0, LANES):
                    mix[lane // LANES, pl.ds(k, 16, stride=8), :] = f[:, lane:lane + LANES]
        o = pl.multiple_of(i * 128, 128)
        for lane in range(0, c0, LANES):
            out_ref[pl.ds(o, 128), lane:lane + LANES] = mix[lane // LANES].astype(BF16)
        logits = lax.dot_general(head_ref[...], out_ref[pl.ds(o, 128), :], (((1,), (1,)), ((), ())),
                                 preferred_element_type=F32)
        logit_ref[:, pl.ds(o, 128)] = logits[0:logit_ref.shape[0]]
        return carry

    lax.fori_loop(0, rows // 16, final, 0)


def unet(g, hot, sw, mask, gain0, gain1, gain2, head, dims, classes):
    rows, c0, c1, c2, offs = dims
    ext = rows + 2 * HALO
    vmem = pl.BlockSpec(memory_space=pltpu.VMEM)
    head = jnp.pad(head.T, ((0, 16 - classes), (0, 0)))
    return pl.pallas_call(
        functools.partial(unet_kernel, dims),
        out_shape=(jax.ShapeDtypeStruct((rows * 8, c0), BF16), jax.ShapeDtypeStruct((classes, rows * 8), F32)),
        in_specs=[pl.BlockSpec(memory_space=pl.ANY)] + [vmem] * 7,
        out_specs=(vmem, vmem),
        scratch_shapes=[
            pltpu.VMEM(g.shape, BF16),
            pltpu.SemaphoreType.DMA((5,)),
            pltpu.VMEM((2, ext, 1024), F32),
            pltpu.VMEM((4, ext + 16, c1), F32),
            pltpu.VMEM((8, ext, c0), BF16),
            pltpu.VMEM((6, rows, c1), BF16),
            pltpu.VMEM((8, ext, c0), BF16),
            pltpu.VMEM((4, ext, c1), BF16),
            pltpu.VMEM((3, rows, c2), BF16),
            pltpu.VMEM((c0 // LANES, 128, LANES), F32),
        ],
        compiler_params=pltpu.CompilerParams(vmem_limit_bytes=64 * 1024 * 1024 - 512 * 1024),
        name="unet",
    )(g, hot, sw, mask, gain0[None], gain1[None], gain2[None], head)


def flat(weight):
    weight = weight.reshape(-1, weight.shape[-1])
    return jnp.pad(weight, ((0, 0), (0, LANES - weight.shape[-1])))


def solution(mesh):
    chips = mesh.shape["seq"] == 8 and mesh.shape["dp"] == 4

    def on_device(bases, stem_weight, stem_gain, first_weight, first_gain, second_weight, second_gain,
                  bottom_project, middle_project, top_project, head_weight):
        weights = (first_weight, second_weight, bottom_project, middle_project, top_project)
        depths = [w.size // w.shape[-1] for w in weights]
        offs = [0]
        for d in depths:
            offs.append(offs[-1] + d)
        if chips and offs[-1] % PIECE == 0:
            g = gather_shards(jnp.concatenate([flat(w) for w in weights], axis=0))
        else:
            parts = []
            for w in weights:
                whole = lax.all_gather(w.reshape(-1, w.shape[-1]), "seq", axis=1, tiled=True)
                whole = whole.reshape(whole.shape[0], 8, -1)
                whole = jnp.pad(whole, ((0, 0), (0, 0), (0, LANES - whole.shape[2])))
                parts.append(whole.reshape(-1, 4, 2 * LANES).transpose(1, 0, 2))
            g = jnp.concatenate(parts, axis=1)

        count = lax.axis_size("seq")
        me = lax.axis_index("seq")
        length = bases.shape[0]
        rows = length // CLASSES
        ext = rows + 2 * HALO
        forward = [(i, i + 1) for i in range(count - 1)]
        low = lax.ppermute(bases[-16:] + 1, "seq", forward) - 1
        high = lax.ppermute(bases[:16] + 1, "seq", [(b, a) for a, b in forward]) - 1
        blank = jnp.full((8 * (HALO + 1) - 16,), -1, jnp.int32)
        line = jnp.concatenate([blank, low, bases, high, blank]).reshape(ext + 2, 8)
        window = jnp.concatenate([line[:-2, 6:], line[1:-1], line[2:, :2]], axis=1)
        lane = jnp.arange(48, dtype=jnp.int32)
        hot = (jnp.repeat(window, 4, axis=1) == (lane % 4)[None]).astype(BF16)
        sw = jnp.stack([jnp.pad(stem_weight, ((4 * r, 28 - 4 * r), (0, 0))) for r in range(8)])
        q = jnp.arange(ext)[:, None]
        outside = ((me == 0) & (q < HALO)) | ((me == count - 1) & (q >= HALO + rows))
        mask = jnp.broadcast_to(jnp.where(outside, 0.0, 1.0).astype(F32), (ext, LANES))
        dims = (rows, stem_weight.shape[1], first_gain.shape[0], second_gain.shape[0], tuple(offs))
        return unet(g, hot, sw, mask, stem_gain, first_gain, second_gain, head_weight, dims, head_weight.shape[1])

    placed = (
        P(("dp", "seq")),
        P(),
        P(),
        P(None, None, "seq"),
        P(),
        P(None, None, "seq"),
        P(),
        P(None, "seq"),
        P(None, "seq"),
        P(None, "seq"),
        P(),
    )
    return jax.shard_map(
        on_device,
        mesh=mesh,
        in_specs=placed,
        out_specs=(P(("dp", "seq"), None), P(None, ("dp", "seq"))),
        check_vma=False,
    )
```

profile of v0, /device:TPU:0, one launch (start us, length us, event | category | flops | bytes accessed | tf_op | source)
XLA Modules:
  0.0 212.4 jit_solution(17211533411977555660)
XLA Ops:
  0.6 0.9 slice_add_fusion
  1.5 1.3 collective-permute-start.1
  2.8 5.5 %collective-permute-start = (s32[16]{0:T(128)S(1)}, s32[16]{0:T(128)S(1)}, u32[]{:S(2)}, u32[]{:S(2)}) collective-permute-start(s32[16]{0:T(128)S(1)} %get-tuple-element.5), channel_id=1, source_target_pairs={{0,4},{4,8},{8,12},{12,16},{16,20},{20,24},{24,28},{1,5},{5,9},{9,... | collective-permute-start | bytes 200 | tf_op jit(solution)/shard_map/ppermute | solution.py:464
  8.3 1.3 broadcast_in_dim.35.gain0_ref
  9.6 1.3 broadcast_in_dim.36.gain1_ref
  10.9 1.1 copy.30
  12.0 1.1 copy.29
  13.1 1.4 bitcast_dynamic-update-slice_fusion.7
  14.5 1.4 bitcast_dynamic-update-slice_fusion.6
  15.9 1.4 bitcast_dynamic-update-slice_fusion.5
  17.3 1.4 bitcast_dynamic-update-slice_fusion.4
  18.7 1.4 bitcast_dynamic-update-slice_fusion.3
  20.1 1.4 bitcast_dynamic-update-slice_fusion.2
  21.5 1.4 bitcast_dynamic-update-slice_fusion.1
  22.9 1.4 bitcast_dynamic-update-slice_fusion.sw_ref
  24.4 1.6 copy.28
  26.0 0.2 pad_dynamic-update-slice_fusion
  26.6 97.3 %gather.1.g_ref = bf16[4,11264,256]{2,1,0:T(8,128)(2,1)S(1)} custom-call(bf16[11264,128]{1,0:T(8,128)(2,1)S(1)} %pad_dynamic-update-slice_fusion.2.x_ref), custom_call_target="tpu_custom_call" | custom-call | bytes 60000000 | tf_op jit(solution)/shard_map/gather/pallas_call | solution.py:197
  123.9 7.7 %copy-done = bf16[4,11264,256]{2,1,0:T(8,128)(2,1)} copy-done((bf16[4,11264,256]{2,1,0:T(8,128)(2,1)}, bf16[4,11264,256]{2,1,0:T(8,128)(2,1)S(1)}, u32[]{:S(2)}) %copy-start) | copy-done | bytes 23068696
  131.6 0.6 pad.59.head_ref
  132.4 0.2 reshape.53
  133.4 0.7 compare_convert_fusion.hot_ref
  134.1 0.8 broadcast_in_dim.34.mask_ref
  134.9 77.5 %unet.1 = (bf16[3072,768]{1,0:T(8,128)(2,1)}, f32[5,3072]{1,0:T(8,128)}) custom-call(bf16[4,11264,256]{2,1,0:T(8,128)(2,1)} %copy-done, bf16[416,48]{1,0:T(8,128)(2,1)} %compare_convert_fusion.hot_ref, bf16[8,48,768]{2,1,0:T(8,128)(2,1)} %bitcast_dynamic-update-slice_fusion.sw_ref, f32[416,128]{1,0:T(8,128)} %broadcast_in_dim.34.mask_ref, ...), custom_call_target="tpu_custom_call" | custom-call | tf_op jit(solution)/shard_map/unet/pallas_call | solution.py:410
  (31 shorter events, 1.3 us)
Async XLA Ops:
  0.6 25.6 %copy-start.1 = (bf16[5,896,128]{2,1,0:T(8,128)(2,1)S(1)}, bf16[5,896,128]{2,1,0:T(8,128)(2,1)}, u32[]{:S(2)}) copy-start(bf16[5,896,128]{2,1,0:T(8,128)(2,1)} %param.16) | copy-start | bytes 3440644
  1.5 130.7 %collective-permute-start.1 = (s32[16]{0:T(128)S(1)}, s32[16]{0:T(128)S(1)}, u32[]{:S(2)}, u32[]{:S(2)}) collective-permute-start(s32[16]{0:T(128)S(1)} %get-tuple-element.4), channel_id=1, source_target_pairs={{4,0},{8,4},{12,8},{16,12},{20,16},{24,20},{28,24},{5,1},{9,5},{13... | collective-permute-start | bytes 200 | tf_op jit(solution)/shard_map/ppermute | solution.py:465
  2.8 129.4 %collective-permute-start = (s32[16]{0:T(128)S(1)}, s32[16]{0:T(128)S(1)}, u32[]{:S(2)}, u32[]{:S(2)}) collective-permute-start(s32[16]{0:T(128)S(1)} %get-tuple-element.5), channel_id=1, source_target_pairs={{0,4},{4,8},{8,12},{12,16},{16,20},{20,24},{24,28},{1,5},{5,9},{9,... | collective-permute-start | bytes 200 | tf_op jit(solution)/shard_map/ppermute | solution.py:464
  24.3 2.0 copy-start.2
  26.6 105.0 %copy-start.4 = (bf16[768,5]{0,1:T(8,128)(2,1)S(1)}, bf16[768,5]{0,1:T(8,128)(2,1)}, u32[]{:S(2)}) copy-start(bf16[768,5]{0,1:T(8,128)(2,1)} %param.21) | copy-start | bytes 23044
  26.6 105.7 %copy-start.3 = (s32[3072]{0:T(1024)S(1)}, s32[3072]{0:T(1024)}, u32[]{:S(2)}) copy-start(s32[3072]{0:T(1024)} %param.11) | copy-start | bytes 36868
  123.9 7.7 %copy-start = (bf16[4,11264,256]{2,1,0:T(8,128)(2,1)}, bf16[4,11264,256]{2,1,0:T(8,128)(2,1)S(1)}, u32[]{:S(2)}) copy-start(bf16[4,11264,256]{2,1,0:T(8,128)(2,1)S(1)} %gather.1.g_ref) | copy-start | bytes 69206016
where the time goes:
time: 213 us; the launch traced here: 212 us
  Pallas kernels  175 us (82%)
  local copies, waits for them, and re-layouts  28.3 us (13%)
  starting transfers between devices  6.78 us (3%)
    pallas_call x1, Pallas kernels, gather_shards(): pl.pallas_call(functools.partial(gather_kernel, pieces), out_shape=jax.Sh...  97.3 us
    pallas_call x1, Pallas kernels, unet(): pl.pallas_call(functools.partial(unet_kernel, dims), out_shape=(jax.Shape...  77.5 us
    unnamed x24, local copies, waits for them, and re-layouts  21.8 us
    ppermute x1, starting transfers between devices, on_device(): low = lax.ppermute(bases[-16:] + 1, 'seq', forward) - 1  5.5 us
  transfers between devices with their start and end apart: 2, of which 0 were waited for; matrix products, arithmetic and copies ran while one was open for 9% of the time, Pallas kernels for 46%

commit v1 on v0

--- a/solution.py
+++ b/solution.py
@@ -17,8 +17,8 @@
 F32 = jnp.float32
 
 
-def gather_kernel(pieces, x_ref, g_ref, local_sem, nat_recv, x_recv, ca_recv, cb_recv,
-                  own_send, nat_send, x_send, ca_send, cb_send):
+def link_steps(pieces, x_ref, g_ref, sems):
+    (local_sem, nat_recv, x_recv, ca_recv, cb_recv, own_send, nat_send, x_send, ca_send, cb_send) = sems
     seq = lax.axis_index("seq")
     dp = lax.axis_index("dp")
     z, y = seq // 2, seq % 2
@@ -108,104 +108,109 @@
         ref = part(k, zz, yy, 1 - x)
         pltpu.make_async_copy(ref, ref, sem.at[k, zz * 2 + yy]).wait()
 
-    def over(body):
-        def step(k, carry):
-            body(k)
-            return carry
-        lax.fori_loop(0, pieces, step, 0)
-
-    def when(cond):
-        return pl.when(cond)
-
-    def first(k):
-        when(z < 3)(lambda: own_copy(k, up_dev, 0).start())
-        when(z > 0)(lambda: own_copy(k, down_dev, 1).start())
+    def start_own(k):
+        pl.when(z < 3)(lambda: own_copy(k, up_dev, 0).start())
+        pl.when(z > 0)(lambda: own_copy(k, down_dev, 1).start())
         own_copy(k, y_dev, 2).start()
 
-    over(first)
-
-    for phase in range(1, 6):
-        def body(k, phase=phase):
-            if phase <= 3:
+    def serve(m):
+        n, i = m // 6, m % 6
+        phase = (6 - i) % 6
+        k = n - phase - jnp.minimum(phase, 1)
+
+        def inside(zz):
+            return jnp.logical_and(zz >= 0, zz < 4)
+
+        @pl.when(jnp.logical_and(k >= 0, k < pieces))
+        def _():
+            @pl.when(phase == 0)
+            def _():
+                start_own(k)
+
+            @pl.when(phase > 0)
+            def _():
                 for sign in (-1, 1):
                     zz = z + sign * phase
 
-                    @pl.when(jnp.logical_and(zz >= 0, zz < 4))
+                    @pl.when(inside(zz))
                     def _(zz=zz, sign=sign):
                         wait_nat(k, zz, y)
                         if sign < 0:
-                            when(z < 3)(lambda: z_copy(k, zz, up_dev).start())
+                            pl.when(z < 3)(lambda: z_copy(k, zz, up_dev).start())
                         else:
-                            when(z > 0)(lambda: z_copy(k, zz, down_dev).start())
+                            pl.when(z > 0)(lambda: z_copy(k, zz, down_dev).start())
                         y_copy(k, zz).start()
                         x_copy(k, zz, y).start()
                         ca_copy(k, zz, y).start()
-            if phase <= 4:
-                for sign in (-1, 1) if phase > 1 else (1,):
+                for sign in (-1, 1):
                     zz = z + sign * (phase - 1)
 
-                    @pl.when(jnp.logical_and(zz >= 0, zz < 4))
+                    @pl.when(jnp.logical_and(inside(zz), phase > (1 if sign < 0 else 0)))
                     def _(zz=zz):
                         wait_nat(k, zz, 1 - y)
                         x_copy(k, zz, 1 - y).start()
                         ca_copy(k, zz, 1 - y).start()
-            late = []
-            if 2 <= phase <= 4:
-                late += [(z - (phase - 1), y), (z + (phase - 1), y)]
-            if phase == 2:
-                late += [(z, 1 - y)]
-            if phase > 2:
-                late += [(z - (phase - 2), 1 - y), (z + (phase - 2), 1 - y)]
-            for zz, yy in late:
-                @pl.when(jnp.logical_and(zz >= 0, zz < 4))
-                def _(zz=zz, yy=yy):
-                    wait_part(k, zz, yy, x_recv)
-                    cb_copy(k, zz, yy).start()
-
-        over(body)
-
-    def last(k):
-        when(z < 3)(lambda: own_copy(k, up_dev, 0).wait_send())
-        when(z > 0)(lambda: own_copy(k, down_dev, 1).wait_send())
-        own_copy(k, y_dev, 2).wait_send()
-        for zz in range(4):
-            @pl.when(zz != z)
-            def _(zz=zz):
-                when(jnp.logical_and(zz < z, z < 3))(lambda: z_copy(k, zz, up_dev).wait_send())
-                when(jnp.logical_and(zz > z, z > 0))(lambda: z_copy(k, zz, down_dev).wait_send())
-                y_copy(k, zz).wait_send()
-            for yy in range(2):
-                @pl.when(zz * 2 + yy != seq)
-                def _(zz=zz, yy=yy):
+                for sign in (-1, 1):
+                    zz = z + sign * (phase - 1)
+
+                    @pl.when(jnp.logical_and(inside(zz), phase > 1))
+                    def _(zz=zz):
+                        wait_part(k, zz, y, x_recv)
+                        cb_copy(k, zz, y).start()
+                for sign in (-1, 1):
+                    zz = z + sign * (phase - 2)
+
+                    @pl.when(jnp.logical_and(inside(zz), phase > (2 if sign < 0 else 1)))
+                    def _(zz=zz):
+                        wait_part(k, zz, 1 - y, x_recv)
+                        cb_copy(k, zz, 1 - y).start()
+
+    def finish(lo, hi):
+        def step(k, carry):
+            def shard(s, carry):
+                @pl.when(s != seq)
+                def _():
+                    zz, yy = s // 2, s % 2
+                    start = k * PIECE + (1 - c) * half
+                    got = slot(zz, yy, start + x * edge, native)
+                    pltpu.make_async_copy(got, got, ca_recv.at[k, s]).wait()
+                    got = slot(zz, yy, start + (1 - x) * native, edge)
+                    pltpu.make_async_copy(got, got, cb_recv.at[k, s]).wait()
+                return carry
+            return lax.fori_loop(0, 8, shard, carry)
+        lax.fori_loop(lo, hi, step, 0)
+
+    def close():
+        def step(k, carry):
+            pl.when(z < 3)(lambda: own_copy(k, up_dev, 0).wait_send())
+            pl.when(z > 0)(lambda: own_copy(k, down_dev, 1).wait_send())
+            own_copy(k, y_dev, 2).wait_send()
+
+            def shard(s, carry):
+                zz, yy = s // 2, s % 2
+
+                @pl.when(s != seq)
+                def _():
                     x_copy(k, zz, yy).wait_send()
                     ca_copy(k, zz, yy).wait_send()
                     cb_copy(k, zz, yy).wait_send()
-                    start = k * PIECE + (1 - c) * half
-                    got = slot(zz, yy, start + x * edge, native)
-                    pltpu.make_async_copy(got, got, ca_recv.at[k, zz * 2 + yy]).wait()
-                    got = slot(zz, yy, start + (1 - x) * native, edge)
-                    pltpu.make_async_copy(got, got, cb_recv.at[k, zz * 2 + yy]).wait()
-
-    over(last)
-    local.wait()
-
-
-def gather_shards(shard):
-    rows = shard.shape[0]
-    pieces = rows // PIECE
+
+                @pl.when(jnp.logical_and(zz != z, yy == 0))
+                def _():
+                    pl.when(jnp.logical_and(zz < z, z < 3))(lambda: z_copy(k, zz, up_dev).wait_send())
+                    pl.when(jnp.logical_and(zz > z, z > 0))(lambda: z_copy(k, zz, down_dev).wait_send())
+                    y_copy(k, zz).wait_send()
+                return carry
+            return lax.fori_loop(0, 8, shard, carry)
+        lax.fori_loop(0, pieces, step, 0)
+
+    return serve, finish, close, local.wait
+
+
+def link_semaphores(pieces):
     dma = pltpu.SemaphoreType.DMA
-    return pl.pallas_call(
-        functools.partial(gather_kernel, pieces),
-        out_shape=jax.ShapeDtypeStruct((4, rows, 2 * LANES), shard.dtype),
-        in_specs=[pl.BlockSpec(memory_space=pl.ANY)],
-        out_specs=pl.BlockSpec(memory_space=pl.ANY),
-        scratch_shapes=[dma, dma((pieces, 8)), dma((pieces, 8)), dma((pieces, 8)), dma((pieces, 8)),
-                        dma((pieces, 3)), dma((pieces, 2, 4)), dma((pieces, 8)), dma((pieces, 8)), dma((pieces, 8))],
-        compiler_params=pltpu.CompilerParams(collective_id=0, has_side_effects=True,
-                                             vmem_limit_bytes=16 * 1024 * 1024),
-        cost_estimate=pl.CostEstimate(flops=0, bytes_accessed=60_000_000, transcendentals=0),
-        name="gather",
-    )(shard)
+    return [dma, dma((pieces, 8)), dma((pieces, 8)), dma((pieces, 8)), dma((pieces, 8)),
+            dma((pieces, 3)), dma((pieces, 2, 4)), dma((pieces, 8)), dma((pieces, 8)), dma((pieces, 8))]
 
 
 def gelu_norm(values, gain, width):
@@ -216,23 +221,54 @@
     return h + h * jnp.tanh(u)
 
 
-def unet_kernel(dims, g_ref, hot_ref, sw_ref, mask_ref, gain0_ref, gain1_ref, gain2_ref, head_ref,
-                out_ref, logit_ref, gv, sems, wide, pf, pb1, pb2, skip0, skip1, skip2, mix):
+def unet_kernel(dims, pieces, g_ref, hot_ref, sw_ref, mask_ref, gain0_ref, gain1_ref, gain2_ref, head_ref,
+                out_ref, logit_ref, gv, sems, wide, pf, pb1, pb2, skip0, skip1, skip2, mix, *links):
     rows, c0, c1, c2, offs = dims
     ext = rows + 2 * HALO
     w0, w1 = c0 // 8, c1 // 8
     cuts = list(zip(offs[:-1], offs[1:]))
 
-    def load(n):
-        lo, hi = cuts[n]
-        return pltpu.make_async_copy(g_ref.at[:, pl.ds(lo, hi - lo), :], gv.at[:, pl.ds(lo, hi - lo), :], sems.at[n])
-
-    for n in range(5):
-        load(n).start()
-
-    def chunks(count, body):
+    if pieces:
+        serve, finish, close, wait_local = link_steps(pieces, g_ref, gv, links)
+    else:
+        def serve(m):
+            return None
+
+        def load(n):
+            lo, hi = cuts[n]
+            return pltpu.make_async_copy(
+                g_ref.at[:, pl.ds(lo, hi - lo), :], gv.at[:, pl.ds(lo, hi - lo), :], sems.at[n])
+
+        for n in range(5):
+            load(n).start()
+
+    served = [0, 0]
+
+    def need(n):
+        if not pieces:
+            load(n).wait()
+            return
+        if served[1] == 0:
+            wait_local()
+        last = min(-(-cuts[n][1] // PIECE), pieces)
+        if last > served[1]:
+            until = (last + 6) * 6
+
+            def step(m, carry):
+                serve(m)
+                return carry
+
+            if until > served[0]:
+                lax.fori_loop(served[0], until, step, 0)
+                served[0] = until
+            finish(served[1], last)
+            served[1] = last
+
+    def chunks(count, body, at=None):
         def step(i, carry):
             body(pl.multiple_of(i * CHUNK, CHUNK))
+            if at is not None:
+                at(i)
             return carry
         lax.fori_loop(0, count // CHUNK, step, 0)
 
@@ -259,10 +295,11 @@
             skip0[2 * j + 1, pl.ds(r, CHUNK), :] = a1.astype(BF16)
             pf[j, pl.ds(r + 8, CHUNK), 0:c0] = 0.5 * (a0 + a1) * mask_ref[pl.ds(r, CHUNK), 0:1]
 
-        chunks(ext, body)
+        chunks(ext, body, lambda i: serve(j * (ext // CHUNK) + i))
         return carry
 
     lax.fori_loop(0, 4, stem, 0)
+    served[0] = 4 * (ext // CHUNK)
 
     where1 = {(k, 0): k for k in range(4)} | {(2, -1): 4, (3, -1): 5, (0, 1): 6, (1, 1): 7}
     for (k, shift), at in where1.items():
@@ -270,12 +307,13 @@
             pb1[at, pl.ds(r, CHUNK), :] = shifted(k, r + 8, shift, c0)
         chunks(ext, body)
 
-    load(0).wait()
+    need(0)
     for j in range(2):
         for e in range(2):
             k = 2 * j + e
 
-            def column(p, carry, k=k, e=e):
+            def column(p, carry, k=k, e=e, m=served[0]):
+                serve(m + p)
                 acc = None
                 for t in range(TAPS):
                     shift, cls = divmod(k + t - 2, 4)
@@ -286,6 +324,7 @@
                 return carry
 
             lax.fori_loop(0, 4, column, 0)
+            served[0] += 4
 
         def body(r, j=j):
             both = []
@@ -297,7 +336,9 @@
                 both.append(a)
             pf[j, pl.ds(r + 8, CHUNK), 0:c1] = 0.5 * (both[0] + both[1]) * mask_ref[pl.ds(r, CHUNK), 0:1]
 
-        chunks(ext, body)
+        first = served[0]
+        chunks(ext, body, lambda i: pl.when(i % 2 == 0)(lambda: serve(first + i // 2)))
+        served[0] += (ext // CHUNK + 1) // 2
 
     where2 = {}
     for k in range(2):
@@ -310,7 +351,7 @@
 
             chunks(rows, body)
 
-    load(1).wait()
+    need(1)
     for e in range(2):
         def column(p, carry, e=e):
             acc = None
@@ -331,7 +372,9 @@
         skip2[1, pl.ds(r, CHUNK), :] = a1.astype(BF16)
         skip2[2, pl.ds(r, CHUNK), :] = (0.5 * (a0 + a1)).astype(BF16)
 
-    chunks(rows, body)
+    first = served[0]
+    chunks(rows, body, lambda i: serve(first + i))
+    served[0] += rows // CHUNK
 
     def lift(slot, lhs, n, depth):
         def column(p, carry):
@@ -340,7 +383,7 @@
             return carry
         lax.fori_loop(0, 4, column, 0)
 
-    load(2).wait()
+    need(2)
     lift(0, lambda: skip2[2], 2, c2)
 
     def body(r):
@@ -350,7 +393,7 @@
 
     chunks(rows, body)
 
-    load(3).wait()
+    need(3)
 
     def middle(j, carry):
         lift(0, lambda: skip2[j], 3, c2)
@@ -367,7 +410,7 @@
 
     lax.fori_loop(0, 2, middle, 0)
 
-    load(4).wait()
+    need(4)
 
     def top(j, carry):
         lift(0, lambda: skip1[j, HALO:HALO + rows, :], 4, c1)
@@ -400,20 +443,22 @@
         return carry
 
     lax.fori_loop(0, rows // 16, final, 0)
-
-
-def unet(g, hot, sw, mask, gain0, gain1, gain2, head, dims, classes):
+    if pieces:
+        close()
+
+
+def unet(g, pieces, hot, sw, mask, gain0, gain1, gain2, head, dims, classes):
     rows, c0, c1, c2, offs = dims
     ext = rows + 2 * HALO
     vmem = pl.BlockSpec(memory_space=pltpu.VMEM)
     head = jnp.pad(head.T, ((0, 16 - classes), (0, 0)))
     return pl.pallas_call(
-        functools.partial(unet_kernel, dims),
+        functools.partial(unet_kernel, dims, pieces),
         out_shape=(jax.ShapeDtypeStruct((rows * 8, c0), BF16), jax.ShapeDtypeStruct((classes, rows * 8), F32)),
         in_specs=[pl.BlockSpec(memory_space=pl.ANY)] + [vmem] * 7,
         out_specs=(vmem, vmem),
         scratch_shapes=[
-            pltpu.VMEM(g.shape, BF16),
+            pltpu.VMEM((4, offs[-1], 2 * LANES), BF16),
             pltpu.SemaphoreType.DMA((5,)),
             pltpu.VMEM((2, ext, 1024), F32),
             pltpu.VMEM((4, ext + 16, c1), F32),
@@ -423,8 +468,10 @@
             pltpu.VMEM((4, ext, c1), BF16),
             pltpu.VMEM((3, rows, c2), BF16),
             pltpu.VMEM((c0 // LANES, 128, LANES), F32),
-        ],
-        compiler_params=pltpu.CompilerParams(vmem_limit_bytes=64 * 1024 * 1024 - 512 * 1024),
+        ] + (link_semaphores(pieces) if pieces else []),
+        compiler_params=pltpu.CompilerParams(
+            **(dict(collective_id=0, has_side_effects=True) if pieces else {}),
+            vmem_limit_bytes=64 * 1024 * 1024 - 512 * 1024),
         name="unet",
     )(g, hot, sw, mask, gain0[None], gain1[None], gain2[None], head)
 
@@ -445,8 +492,10 @@
         for d in depths:
             offs.append(offs[-1] + d)
         if chips and offs[-1] % PIECE == 0:
-            g = gather_shards(jnp.concatenate([flat(w) for w in weights], axis=0))
+            pieces = offs[-1] // PIECE
+            g = jnp.concatenate([flat(w) for w in weights], axis=0)
         else:
+            pieces = 0
             parts = []
             for w in weights:
                 whole = lax.all_gather(w.reshape(-1, w.shape[-1]), "seq", axis=1, tiled=True)
@@ -468,12 +517,14 @@
         window = jnp.concatenate([line[:-2, 6:], line[1:-1], line[2:, :2]], axis=1)
         lane = jnp.arange(48, dtype=jnp.int32)
         hot = (jnp.repeat(window, 4, axis=1) == (lane % 4)[None]).astype(BF16)
-        sw = jnp.stack([jnp.pad(stem_weight, ((4 * r, 28 - 4 * r), (0, 0))) for r in range(8)])
+        at = jnp.arange(8 * 48, dtype=jnp.int32)[:, None]
+        pick = (at % 48 - 4 * (at // 48) == jnp.arange(20, dtype=jnp.int32)[None]).astype(BF16)
+        sw = jnp.dot(pick, stem_weight, preferred_element_type=F32).astype(BF16).reshape(8, 48, -1)
         q = jnp.arange(ext)[:, None]
         outside = ((me == 0) & (q < HALO)) | ((me == count - 1) & (q >= HALO + rows))
         mask = jnp.broadcast_to(jnp.where(outside, 0.0, 1.0).astype(F32), (ext, LANES))
         dims = (rows, stem_weight.shape[1], first_gain.shape[0], second_gain.shape[0], tuple(offs))
-        return unet(g, hot, sw, mask, stem_gain, first_gain, second_gain, head_weight, dims, head_weight.shape[1])
+        return unet(g, pieces, hot, sw, mask, stem_gain, first_gain, second_gain, head_weight, dims, head_weight.shape[1])
 
     placed = (
         P(("dp", "seq")),

time: 213 us -> 176 us (0.83)
  Pallas kernels: 175 us -> 146 us
  local copies, waits for them, and re-layouts: 28.3 us -> 18.8 us
    pallas_call x2 -> x1, Pallas kernels: 175 us -> 146 us  [unet(): pl.pallas_call(functools.partial(unet_kernel, dims, pieces), out_shape=(j...]
    unnamed x24 -> x21, local copies, waits for them, and re-layouts: 21.8 us -> 13 us
  transfers between devices with their start and end apart: 2 -> 2, of which waited for: 0 -> 0; matrix products, arithmetic and copies ran while one was open for 9% -> 7% of each run, Pallas kernels for 46% -> 0%
where the time goes in v1:
time: 176 us
  Pallas kernels  146 us (83%)
  local copies, waits for them, and re-layouts  18.8 us (11%)
  starting transfers between devices  6.78 us (4%)
    pallas_call x1, Pallas kernels, unet(): pl.pallas_call(functools.partial(unet_kernel, dims, pieces), out_shape=(j...  146 us
    unnamed x21, local copies, waits for them, and re-layouts  13 us
    ppermute x1, starting transfers between devices, on_device(): low = lax.ppermute(bases[-16:] + 1, 'seq', forward) - 1  5.5 us
  transfers between devices with their start and end apart: 2, of which 0 were waited for; matrix products, arithmetic and copies ran while one was open for 7% of the time, Pallas kernels for 0%

profile of v1, /device:TPU:0, one launch (start us, length us, event | category | flops | bytes accessed | tf_op | source)
XLA Modules:
  0.0 175.6 jit_solution(3315432959808594081)
XLA Ops:
  0.7 0.9 slice_add_fusion
  1.5 1.3 collective-permute-start.1
  2.8 5.5 %collective-permute-start = (s32[16]{0:T(128)S(1)}, s32[16]{0:T(128)S(1)}, u32[]{:S(2)}, u32[]{:S(2)}) collective-permute-start(s32[16]{0:T(128)S(1)} %get-tuple-element.5), channel_id=1, source_target_pairs={{0,4},{4,8},{8,12},{12,16},{16,20},{20,24},{24,28},{1,5},{5,9},{9,... | collective-permute-start | bytes 200 | tf_op jit(solution)/shard_map/ppermute | solution.py:513
  8.4 1.3 broadcast_in_dim.37.gain0_ref
  9.6 1.3 broadcast_in_dim.38.gain1_ref
  10.9 1.1 copy.30
  12.0 1.1 copy.29
  13.1 1.6 copy.28
  14.7 1.1 pad_dynamic-update-slice_fusion
  15.9 1.2 convolution_convert_fusion
  17.1 1.1 constant_dynamic-update-slice_fusion.1
  18.2 0.7 constant_dynamic-update-slice_fusion
  18.9 0.8 pad_dynamic-update-slice_fusion.1
  19.6 0.7 pad_dynamic-update-slice_fusion.2.g_ref
  20.4 0.6 pad.19.head_ref
  21.2 0.2 reshape.94
  21.4 0.1 slice.30
  21.6 0.1 fusion.14
  22.1 0.1 copy.34
  22.2 0.7 compare_convert_fusion.hot_ref
  22.9 0.8 broadcast_in_dim.36.mask_ref
  23.7 146.4 %unet.1 = (bf16[3072,768]{1,0:T(8,128)(2,1)}, f32[5,3072]{1,0:T(8,128)}) custom-call(bf16[11264,128]{1,0:T(8,128)(2,1)} %pad_dynamic-update-slice_fusion.2.g_ref, bf16[416,48]{1,0:T(8,128)(2,1)} %compare_convert_fusion.hot_ref, bf16[8,48,768]{2,1,0:T(8,128)(2,1)} %bitcast.9, f32[416,128]{1,0:T(8,128)} %broadcast_in_dim.36.mask_ref, ...), custom_call_target="tpu_custom_call" | custom-call | tf_op jit(solution)/shard_map/unet/pallas_call | solution.py:455
  170.1 4.9 %copy.42 = bf16[3072,768]{1,0:T(8,128)(2,1)} copy(bf16[3072,768]{1,0:T(8,128)(2,1)} %get-tuple-element.8) | data formatting | bytes 9437184
  175.0 0.6 copy.43
  (28 shorter events, 0.6 us)
Async XLA Ops:
  0.6 15.3 %copy-start = (bf16[20,768]{1,0:T(8,128)(2,1)S(1)}, bf16[20,768]{1,0:T(8,128)(2,1)}, u32[]{:S(2)}) copy-start(bf16[20,768]{1,0:T(8,128)(2,1)} %param.12) | copy-start | bytes 92164
  0.6 16.4 %copy-start.1 = (bf16[5,896,128]{2,1,0:T(8,128)(2,1)S(1)}, bf16[5,896,128]{2,1,0:T(8,128)(2,1)}, u32[]{:S(2)}) copy-start(bf16[5,896,128]{2,1,0:T(8,128)(2,1)} %param.16) | copy-start | bytes 3440644
  1.5 19.5 %collective-permute-start.1 = (s32[16]{0:T(128)S(1)}, s32[16]{0:T(128)S(1)}, u32[]{:S(2)}, u32[]{:S(2)}) collective-permute-start(s32[16]{0:T(128)S(1)} %get-tuple-element.4), channel_id=1, source_target_pairs={{4,0},{8,4},{12,8},{16,12},{20,16},{24,20},{28,24},{5,1},{9,5},{13... | collective-permute-start | bytes 200 | tf_op jit(solution)/shard_map/ppermute | solution.py:514
  2.8 18.2 %collective-permute-start = (s32[16]{0:T(128)S(1)}, s32[16]{0:T(128)S(1)}, u32[]{:S(2)}, u32[]{:S(2)}) collective-permute-start(s32[16]{0:T(128)S(1)} %get-tuple-element.5), channel_id=1, source_target_pairs={{0,4},{4,8},{8,12},{12,16},{16,20},{20,24},{24,28},{1,5},{5,9},{9,... | collective-permute-start | bytes 200 | tf_op jit(solution)/shard_map/ppermute | solution.py:513
  14.7 3.5 %copy-start.2 = (bf16[1024,128]{1,0:T(8,128)(2,1)S(1)}, bf16[1024,128]{1,0:T(8,128)(2,1)}, u32[]{:S(2)}) copy-start(bf16[1024,128]{1,0:T(8,128)(2,1)} %param.18) | copy-start | bytes 786436
  14.7 5.7 %copy-start.5 = (bf16[768,5]{0,1:T(8,128)(2,1)S(1)}, bf16[768,5]{0,1:T(8,128)(2,1)}, u32[]{:S(2)}) copy-start(bf16[768,5]{0,1:T(8,128)(2,1)} %param.21) | copy-start | bytes 23044
  14.7 6.3 %copy-start.4 = (s32[3072]{0:T(1024)S(1)}, s32[3072]{0:T(1024)}, u32[]{:S(2)}) copy-start(s32[3072]{0:T(1024)} %param.11) | copy-start | bytes 36868
  170.1 4.9 %copy-start.3 = (f32[5,3072]{1,0:T(8,128)S(1)}, f32[5,3072]{1,0:T(8,128)}, u32[]{:S(2)}) copy-start(f32[5,3072]{1,0:T(8,128)} %get-tuple-element.9) | copy-start | bytes 184324

commit v2 on v1

--- a/solution.py
+++ b/solution.py
@@ -13,6 +13,8 @@
 CHUNK = 32
 LANES = 128
 PIECE = 1024
+AHEAD = 1
+SPLIT = 1
 BF16 = jnp.bfloat16
 F32 = jnp.float32
 
@@ -23,7 +25,9 @@
     dp = lax.axis_index("dp")
     z, y = seq // 2, seq % 2
     x, c = dp // 2, dp % 2
-    half, edge, native = PIECE // 2, 3 * PIECE // 16, 5 * PIECE // 16
+    half = PIECE // 2
+    edge = half * 3 // 8 // 16 * 16
+    native = half - edge
 
     def there(zz, yy, xx, cc):
         return {"seq": zz * 2 + yy, "dp": xx * 2 + cc}
@@ -57,7 +61,7 @@
         pl.semaphore_wait(barrier, 4)
 
     def slot(zz, yy, start, count):
-        return g_ref.at[zz, pl.ds(pl.multiple_of(start, 64), count),
+        return g_ref.at[zz, pl.ds(pl.multiple_of(start, 16), count),
                         pl.ds(pl.multiple_of(yy * LANES, LANES), LANES)]
 
     def base(k):
@@ -74,7 +78,7 @@
         return slot(zz, yy, base(k) + xx * native, edge)
 
     def own_copy(k, dev, which):
-        src = x_ref.at[pl.ds(pl.multiple_of(base(k) + x * edge, 64), native), :]
+        src = x_ref.at[pl.ds(pl.multiple_of(base(k) + x * edge, 16), native), :]
         return copy(src, nat(k, z, y), own_send.at[k, which], nat_recv.at[k, seq], dev)
 
     def z_copy(k, zz, dev):
@@ -116,7 +120,7 @@
     def serve(m):
         n, i = m // 6, m % 6
         phase = (6 - i) % 6
-        k = n - phase - jnp.minimum(phase, 1)
+        k = n - phase - AHEAD * jnp.minimum(phase, 1)
 
         def inside(zz):
             return jnp.logical_and(zz >= 0, zz < 4)
@@ -180,7 +184,7 @@
             return lax.fori_loop(0, 8, shard, carry)
         lax.fori_loop(lo, hi, step, 0)
 
-    def close():
+    def close(lo, hi):
         def step(k, carry):
             pl.when(z < 3)(lambda: own_copy(k, up_dev, 0).wait_send())
             pl.when(z > 0)(lambda: own_copy(k, down_dev, 1).wait_send())
@@ -202,7 +206,7 @@
                     y_copy(k, zz).wait_send()
                 return carry
             return lax.fori_loop(0, 8, shard, carry)
-        lax.fori_loop(0, pieces, step, 0)
+        lax.fori_loop(lo, hi, step, 0)
 
     return serve, finish, close, local.wait
 
@@ -221,7 +225,7 @@
     return h + h * jnp.tanh(u)
 
 
-def unet_kernel(dims, pieces, g_ref, hot_ref, sw_ref, mask_ref, gain0_ref, gain1_ref, gain2_ref, head_ref,
+def unet_kernel(dims, pieces, g_ref, hot_ref, sw_ref, gain_ref, head_ref,
                 out_ref, logit_ref, gv, sems, wide, pf, pb1, pb2, skip0, skip1, skip2, mix, *links):
     rows, c0, c1, c2, offs = dims
     ext = rows + 2 * HALO
@@ -229,7 +233,18 @@
     cuts = list(zip(offs[:-1], offs[1:]))
 
     if pieces:
-        serve, finish, close, wait_local = link_steps(pieces, g_ref, gv, links)
+        serve_one, finish, close, wait_local = link_steps(pieces, g_ref, gv, links)
+
+        def serve(m):
+            if SPLIT == 1:
+                serve_one(m)
+                return
+
+            def one(i, carry):
+                serve_one(m * SPLIT + i)
+                return carry
+
+            lax.fori_loop(0, SPLIT, one, 0)
     else:
         def serve(m):
             return None
@@ -242,7 +257,7 @@
         for n in range(5):
             load(n).start()
 
-    served = [0, 0]
+    served = [0, 0, 0]
 
     def need(n):
         if not pieces:
@@ -250,9 +265,12 @@
             return
         if served[1] == 0:
             wait_local()
+        elif n <= 2:
+            close(served[2], served[1])
+            served[2] = served[1]
         last = min(-(-cuts[n][1] // PIECE), pieces)
         if last > served[1]:
-            until = (last + 6) * 6
+            until = -(-(last + 5 + AHEAD) * 6 // SPLIT)
 
             def step(m, carry):
                 serve(m)
@@ -272,6 +290,14 @@
             return carry
         lax.fori_loop(0, count // CHUNK, step, 0)
 
+    me = lax.axis_index("seq")
+    low = jnp.where(me == 0, HALO, 0)
+    high = jnp.where(me == lax.axis_size("seq") - 1, HALO + rows, ext)
+
+    def inside(r):
+        at = r + lax.broadcasted_iota(jnp.int32, (CHUNK, 1), 0)
+        return jnp.where(jnp.logical_and(at >= low, at < high), 1.0, 0.0)
+
     def shifted(k, start, shift, width):
         if shift == 0:
             return pf[k, pl.ds(start, CHUNK), 0:width].astype(BF16)
@@ -289,11 +315,11 @@
             wide[e, :, 0:c0] = jnp.dot(hot_ref[...], sw_ref[2 * j + e], preferred_element_type=F32)
 
         def body(r):
-            a0 = gelu_norm(wide[0, pl.ds(r, CHUNK), 0:c0], gain0_ref[...], c0)
-            a1 = gelu_norm(wide[1, pl.ds(r, CHUNK), 0:c0], gain0_ref[...], c0)
+            a0 = gelu_norm(wide[0, pl.ds(r, CHUNK), 0:c0], gain_ref[:, 0:c0], c0)
+            a1 = gelu_norm(wide[1, pl.ds(r, CHUNK), 0:c0], gain_ref[:, 0:c0], c0)
             skip0[2 * j, pl.ds(r, CHUNK), :] = a0.astype(BF16)
             skip0[2 * j + 1, pl.ds(r, CHUNK), :] = a1.astype(BF16)
-            pf[j, pl.ds(r + 8, CHUNK), 0:c0] = 0.5 * (a0 + a1) * mask_ref[pl.ds(r, CHUNK), 0:1]
+            pf[j, pl.ds(r + 8, CHUNK), 0:c0] = 0.5 * (a0 + a1) * inside(r)
 
         chunks(ext, body, lambda i: serve(j * (ext // CHUNK) + i))
         return carry
@@ -331,10 +357,10 @@
             for e in range(2):
                 row = wide[e, pl.ds(r, CHUNK), :]
                 row = jnp.concatenate([row[:, s * LANES:s * LANES + w1] for s in range(8)], axis=1)
-                a = gelu_norm(row, gain1_ref[...], c1)
+                a = gelu_norm(row, gain_ref[:, c0:c0 + c1], c1)
                 skip1[2 * j + e, pl.ds(r, CHUNK), :] = a.astype(BF16)
                 both.append(a)
-            pf[j, pl.ds(r + 8, CHUNK), 0:c1] = 0.5 * (both[0] + both[1]) * mask_ref[pl.ds(r, CHUNK), 0:1]
+            pf[j, pl.ds(r + 8, CHUNK), 0:c1] = 0.5 * (both[0] + both[1]) * inside(r)
 
         first = served[0]
         chunks(ext, body, lambda i: pl.when(i % 2 == 0)(lambda: serve(first + i // 2)))
@@ -366,8 +392,8 @@
         lax.fori_loop(0, 4, column, 0)
 
     def body(r):
-        a0 = gelu_norm(wide[0, pl.ds(r, CHUNK), :], gain2_ref[...], c2)
-        a1 = gelu_norm(wide[1, pl.ds(r, CHUNK), :], gain2_ref[...], c2)
+        a0 = gelu_norm(wide[0, pl.ds(r, CHUNK), :], gain_ref[:, c0 + c1:c0 + c1 + c2], c2)
+        a1 = gelu_norm(wide[1, pl.ds(r, CHUNK), :], gain_ref[:, c0 + c1:c0 + c1 + c2], c2)
         skip2[0, pl.ds(r, CHUNK), :] = a0.astype(BF16)
         skip2[1, pl.ds(r, CHUNK), :] = a1.astype(BF16)
         skip2[2, pl.ds(r, CHUNK), :] = (0.5 * (a0 + a1)).astype(BF16)
@@ -444,10 +470,10 @@
 
     lax.fori_loop(0, rows // 16, final, 0)
     if pieces:
-        close()
-
-
-def unet(g, pieces, hot, sw, mask, gain0, gain1, gain2, head, dims, classes):
+        close(served[2], pieces)
+
+
+def unet(g, pieces, hot, sw, gains, head, dims, classes):
     rows, c0, c1, c2, offs = dims
     ext = rows + 2 * HALO
     vmem = pl.BlockSpec(memory_space=pltpu.VMEM)
@@ -455,7 +481,7 @@
     return pl.pallas_call(
         functools.partial(unet_kernel, dims, pieces),
         out_shape=(jax.ShapeDtypeStruct((rows * 8, c0), BF16), jax.ShapeDtypeStruct((classes, rows * 8), F32)),
-        in_specs=[pl.BlockSpec(memory_space=pl.ANY)] + [vmem] * 7,
+        in_specs=[pl.BlockSpec(memory_space=pl.ANY)] + [vmem] * 4,
         out_specs=(vmem, vmem),
         scratch_shapes=[
             pltpu.VMEM((4, offs[-1], 2 * LANES), BF16),
@@ -473,7 +499,7 @@
             **(dict(collective_id=0, has_side_effects=True) if pieces else {}),
             vmem_limit_bytes=64 * 1024 * 1024 - 512 * 1024),
         name="unet",
-    )(g, hot, sw, mask, gain0[None], gain1[None], gain2[None], head)
+    )(g, hot, sw, gains[None], head)
 
 
 def flat(weight):
@@ -505,7 +531,6 @@
             g = jnp.concatenate(parts, axis=1)
 
         count = lax.axis_size("seq")
-        me = lax.axis_index("seq")
         length = bases.shape[0]
         rows = length // CLASSES
         ext = rows + 2 * HALO
@@ -520,11 +545,9 @@
         at = jnp.arange(8 * 48, dtype=jnp.int32)[:, None]
         pick = (at % 48 - 4 * (at // 48) == jnp.arange(20, dtype=jnp.int32)[None]).astype(BF16)
         sw = jnp.dot(pick, stem_weight, preferred_element_type=F32).astype(BF16).reshape(8, 48, -1)
-        q = jnp.arange(ext)[:, None]
-        outside = ((me == 0) & (q < HALO)) | ((me == count - 1) & (q >= HALO + rows))
-        mask = jnp.broadcast_to(jnp.where(outside, 0.0, 1.0).astype(F32), (ext, LANES))
         dims = (rows, stem_weight.shape[1], first_gain.shape[0], second_gain.shape[0], tuple(offs))
-        return unet(g, pieces, hot, sw, mask, stem_gain, first_gain, second_gain, head_weight, dims, head_weight.shape[1])
+        gains = jnp.concatenate([stem_gain, first_gain, second_gain])
+        return unet(g, pieces, hot, sw, gains, head_weight, dims, head_weight.shape[1])
 
     placed = (
         P(("dp", "seq")),

time: 176 us -> 174 us (0.989)
  local copies, waits for them, and re-layouts: 18.8 us -> 16 us
    broadcast_in_dim x3 -> x1, local copies, waits for them, and re-layouts: 3.37 us -> 0.6 us  [unet(): gains[None]]
where the time goes in v2:
time: 174 us
  Pallas kernels  146 us (84%)
  local copies, waits for them, and re-layouts  16 us (9%)
  starting transfers between devices  6.78 us (4%)
  other arithmetic  2.32 us (1%)
    pallas_call x1, Pallas kernels, unet(): pl.pallas_call(functools.partial(unet_kernel, dims, pieces), out_shape=(j...  146 us
    unnamed x21, local copies, waits for them, and re-layouts  13 us
    ppermute x1, starting transfers between devices, on_device(): low = lax.ppermute(bases[-16:] + 1, 'seq', forward) - 1  5.5 us
  transfers between devices with their start and end apart: 2, of which 0 were waited for; matrix products, arithmetic and copies ran while one was open for 7% of the time, Pallas kernels for 0%

profile of v2, /device:TPU:0, one launch (start us, length us, event | category | flops | bytes accessed | tf_op | source)
XLA Modules:
  0.0 173.5 jit_solution(9849815877201214052)
XLA Ops:
  0.7 0.9 slice_add_fusion
  1.5 1.3 collective-permute-start.1
  2.8 5.5 %collective-permute-start = (s32[16]{0:T(128)S(1)}, s32[16]{0:T(128)S(1)}, u32[]{:S(2)}, u32[]{:S(2)}) collective-permute-start(s32[16]{0:T(128)S(1)} %get-tuple-element.5), channel_id=1, source_target_pairs={{0,4},{4,8},{8,12},{12,16},{16,20},{20,24},{24,28},{1,5},{5,9},{9,... | collective-permute-start | bytes 200 | tf_op jit(solution)/shard_map/ppermute | solution.py:538
  8.4 0.7 pad_maximum_fusion
  9.1 0.6 broadcast_in_dim.14.gain_ref
  9.7 1.1 copy.30
  10.8 1.1 copy.29
  11.9 1.6 copy.28
  13.5 1.1 pad_dynamic-update-slice_fusion
  14.7 1.2 convolution_convert_fusion
  15.8 1.1 constant_dynamic-update-slice_fusion.1
  16.9 0.7 constant_dynamic-update-slice_fusion
  17.6 0.8 pad_dynamic-update-slice_fusion.1
  18.4 0.7 pad_dynamic-update-slice_fusion.2.g_ref
  19.1 0.6 pad.19.head_ref
  20.0 0.2 reshape.77
  20.1 0.1 slice.30
  20.4 0.1 fusion.10
  20.6 0.1 copy.33
  20.8 0.1 copy.34
  21.0 0.7 compare_convert_fusion.hot_ref
  21.6 146.4 %unet.1 = (bf16[3072,768]{1,0:T(8,128)(2,1)}, f32[5,3072]{1,0:T(8,128)}) custom-call(bf16[11264,128]{1,0:T(8,128)(2,1)} %pad_dynamic-update-slice_fusion.2.g_ref, bf16[416,48]{1,0:T(8,128)(2,1)} %compare_convert_fusion.hot_ref, bf16[8,48,768]{2,1,0:T(8,128)(2,1)} %bitcast.8, f32[1,2688]{1,0:T(1,128)} %broadcast_in_dim.14.gain_ref, bf16[16,768]{1,0:T(8,128)(2,1)} %pad.19.head_ref), custom_call_target="tpu_custom_call" | custom-call | tf_op jit(solution)/shard_map/unet/pallas_call | solution.py:481
  168.0 4.9 %copy.42 = bf16[3072,768]{1,0:T(8,128)(2,1)} copy(bf16[3072,768]{1,0:T(8,128)(2,1)} %get-tuple-element.8) | data formatting | bytes 9437184
  172.9 0.6 copy.43
  (26 shorter events, 0.5 us)
Async XLA Ops:
  0.6 14.0 %copy-start = (bf16[20,768]{1,0:T(8,128)(2,1)S(1)}, bf16[20,768]{1,0:T(8,128)(2,1)}, u32[]{:S(2)}) copy-start(bf16[20,768]{1,0:T(8,128)(2,1)} %param.12) | copy-start | bytes 92164
  0.6 15.2 %copy-start.1 = (bf16[5,896,128]{2,1,0:T(8,128)(2,1)S(1)}, bf16[5,896,128]{2,1,0:T(8,128)(2,1)}, u32[]{:S(2)}) copy-start(bf16[5,896,128]{2,1,0:T(8,128)(2,1)} %param.16) | copy-start | bytes 3440644
  1.5 18.2 %collective-permute-start.1 = (s32[16]{0:T(128)S(1)}, s32[16]{0:T(128)S(1)}, u32[]{:S(2)}, u32[]{:S(2)}) collective-permute-start(s32[16]{0:T(128)S(1)} %get-tuple-element.4), channel_id=1, source_target_pairs={{4,0},{8,4},{12,8},{16,12},{20,16},{24,20},{28,24},{5,1},{9,5},{13... | collective-permute-start | bytes 200 | tf_op jit(solution)/shard_map/ppermute | solution.py:539
  2.8 16.9 %collective-permute-start = (s32[16]{0:T(128)S(1)}, s32[16]{0:T(128)S(1)}, u32[]{:S(2)}, u32[]{:S(2)}) collective-permute-start(s32[16]{0:T(128)S(1)} %get-tuple-element.5), channel_id=1, source_target_pairs={{0,4},{4,8},{8,12},{12,16},{16,20},{20,24},{24,28},{1,5},{5,9},{9,... | collective-permute-start | bytes 200 | tf_op jit(solution)/shard_map/ppermute | solution.py:538
  13.5 3.5 %copy-start.2 = (bf16[1024,128]{1,0:T(8,128)(2,1)S(1)}, bf16[1024,128]{1,0:T(8,128)(2,1)}, u32[]{:S(2)}) copy-start(bf16[1024,128]{1,0:T(8,128)(2,1)} %param.18) | copy-start | bytes 786436
  13.5 5.7 %copy-start.5 = (bf16[768,5]{0,1:T(8,128)(2,1)S(1)}, bf16[768,5]{0,1:T(8,128)(2,1)}, u32[]{:S(2)}) copy-start(bf16[768,5]{0,1:T(8,128)(2,1)} %param.21) | copy-start | bytes 23044
  13.5 6.3 %copy-start.4 = (s32[3072]{0:T(1024)S(1)}, s32[3072]{0:T(1024)}, u32[]{:S(2)}) copy-start(s32[3072]{0:T(1024)} %param.11) | copy-start | bytes 36868
  168.0 4.9 %copy-start.3 = (f32[5,3072]{1,0:T(8,128)S(1)}, f32[5,3072]{1,0:T(8,128)}, u32[]{:S(2)}) copy-start(f32[5,3072]{1,0:T(8,128)} %get-tuple-element.9) | copy-start | bytes 184324
